TPU v7x, 128 devices: a whole 4x4x4 slice. The times are simulated.
128 devices in a mesh: section: 2 (over core), dp: 16 (over y, x), tensor: 4 (over z).
Axes of the slice: x: 4, y: 4, z: 4, core: 2. Of those that a mesh axis runs over, the one named last changes fastest.
Arguments:
- boundary_copies: bfloat16 [2, 2, 32, 128, 4096], P('section', None, 'dp', None, 'tensor'), may hold values from -6 to 6
- arriving: bfloat16 [2, 16, 128, 4096], P('section', 'dp', None, 'tensor'), may hold values from -7 to 7
- first_delta: bfloat16 [2, 16, 128, 4096], P(None, 'dp', None, 'tensor'), may hold values from -7 to 7
- sample_index: int32 [4, 16], P(None, 'dp'), may hold values from 0 to 1
- exponents: int32 [3, 32], P(None, 'tensor'), may hold values from -3 to -1
- norm_gain: float32 [2, 4096], P('section'), may hold values from 0.25 to 1.75
- w_query: bfloat16 [2, 4096, 4096], P('section', 'dp', 'tensor'), may hold values from -0.09375 to 0.09375
- w_key: bfloat16 [2, 4096, 512], P('section', 'dp', 'tensor'), may hold values from -0.09375 to 0.09375
- w_value: bfloat16 [2, 4096, 512], P('section', 'dp', 'tensor'), may hold values from -0.09375 to 0.09375
- w_out: bfloat16 [2, 4096, 4096], P('section', 'tensor', 'dp'), may hold values from -0.09375 to 0.09375
- out_grad: bfloat16 [2, 3, 16, 128, 4096], P('section', None, 'dp'), may hold values from -6 to 6
Outputs:
- copies_new: bfloat16 [2, 2, 32, 128, 4096], P('section', None, 'dp', None, 'tensor')
- grad_query: bfloat16 [2, 4096, 4096], P('section', 'dp', 'tensor')
- grad_value: bfloat16 [2, 4096, 512], P('section', 'dp', 'tensor')
All inputs are finite; a program needn't handle non-finite values.
Results may differ from a plain program's by a relative error of at most 0.025.
Values may be sent and summed in bfloat16 or wider, within the bound.
No kernel may reach another device: no remote copies, remote signals or barrier semaphores. Data moves between devices by JAX's collectives and lax.ppermute only.
A program may use at most 128 MiB of HBM per device.

v0:
```python
import jax
import jax.numpy as jnp
from jax import lax
from jax.sharding import PartitionSpec as P

HQ = 32
HK = 4
HD = 128
QB = 128


eps_norm = 1e-05
qmax = 7.0


def passed_along(shard, axis, by):
    count = lax.axis_size(axis)
    pairs = [(i, i + by) for i in range(count) if 0 <= i + by < count]
    return lax.ppermute(shard, axis, pairs)


def normalize(inputs, gain):
    values = inputs.astype(jnp.float32)
    square = jnp.mean(values * values, axis=-1, keepdims=True)
    return (values * lax.rsqrt(square + eps_norm) * gain).astype(jnp.bfloat16)


def attend(query, key_in, value_in):
    length = query.shape[0]
    group = HQ // HK
    scale = HD ** (-0.5)
    q_heads = query.reshape(length, -1, group, HD)
    k_heads = key_in.reshape(length, -1, HD)
    v_heads = value_in.reshape(length, -1, HD)
    scores = (
        jnp.einsum("sngd,tnd->ngst", q_heads, k_heads, preferred_element_type=jnp.float32) * scale
    )
    causal = jnp.arange(length)[:, None] >= jnp.arange(length)[None, :]
    scores = jnp.where(causal, scores, -1e30)
    probs = jax.nn.softmax(scores, axis=-1)
    rounded = probs.astype(jnp.bfloat16)
    mixed = jnp.einsum(
        "ngst,tnd->sngd", rounded, v_heads, preferred_element_type=jnp.float32
    ).reshape(length, -1)
    return (mixed.astype(jnp.bfloat16), probs, rounded)


def attend_back(query, key_in, value_in, probs, rounded, d_mixed):
    length = query.shape[0]
    group = HQ // HK
    scale = HD ** (-0.5)
    k_heads = key_in.astype(jnp.float32).reshape(length, -1, HD)
    v_heads = value_in.reshape(length, -1, HD)
    d_heads = d_mixed.reshape(length, -1, group, HD)
    d_probs = jnp.einsum("sngd,tnd->ngst", d_heads, v_heads, preferred_element_type=jnp.float32)
    d_scores = probs * (d_probs - jnp.sum(d_probs * probs, axis=-1, keepdims=True)) * scale
    d_query = jnp.einsum("ngst,tnd->sngd", d_scores, k_heads).reshape(length, -1)
    d_value = jnp.einsum(
        "ngst,sngd->tnd", rounded, d_heads, preferred_element_type=jnp.float32
    ).reshape(length, -1)
    return (d_query.astype(jnp.bfloat16), d_value.astype(jnp.bfloat16))


def local_term(left, right):
    return lax.dot_general(
        left, right, (((0,), (0,)), ((), ())), preferred_element_type=jnp.float32
    )


def on_device(
    boundary_copies,
    arriving,
    first_delta,
    sample_index,
    exponents,
    norm_gain,
    w_query,
    w_key,
    w_value,
    w_out,
    out_grad,
):
    section = lax.axis_index("section")
    sections = lax.axis_size("section")
    ticks = out_grad.shape[1]
    full_q, full_k, full_v, full_o = (
        lax.all_gather(w_query[0], "dp", axis=0, tiled=True),
        lax.all_gather(w_key[0], "dp", axis=0, tiled=True),
        lax.all_gather(w_value[0], "dp", axis=0, tiled=True),
        lax.all_gather(w_out[0], "dp", axis=1, tiled=True),
    )
    power = exponents.astype(jnp.float32)
    scale_full = jnp.repeat(jnp.exp2(power), QB, axis=1)
    inverse_full = jnp.repeat(jnp.exp2(-power), QB, axis=1)
    scale_in = lax.dynamic_index_in_dim(scale_full, section, 0, keepdims=False)
    scale_next = lax.dynamic_index_in_dim(scale_full, section + 1, 0, keepdims=False)
    inverse_next = lax.dynamic_index_in_dim(inverse_full, section + 1, 0, keepdims=False)
    copy_in = boundary_copies[0, 0]
    copy_out = boundary_copies[0, 1]
    gain = norm_gain[0]
    slots = sample_index[:, 0]
    delta = arriving[0, 0]
    passed = delta
    kept_normed, kept_dq, kept_dv = ([], [], [])
    for tick in range(ticks):
        if tick > 0:
            delta = jnp.where(section == 0, first_delta[tick - 1, 0], passed)
        micro = tick - section + sections - 1
        slot = lax.dynamic_index_in_dim(slots, micro, 0, keepdims=False)
        old_in = lax.dynamic_index_in_dim(copy_in, slot, 0, keepdims=False)
        inputs = (old_in.astype(jnp.float32) + scale_in * delta.astype(jnp.float32)).astype(
            jnp.bfloat16
        )
        copy_in = lax.dynamic_update_index_in_dim(copy_in, inputs, slot, 0)
        whole = lax.all_gather(inputs, "tensor", axis=1, tiled=True)
        normed = normalize(whole, gain)
        query = jnp.dot(normed, full_q, preferred_element_type=jnp.float32).astype(jnp.bfloat16)
        key_in = jnp.dot(normed, full_k, preferred_element_type=jnp.float32).astype(jnp.bfloat16)
        value_in = jnp.dot(normed, full_v, preferred_element_type=jnp.float32).astype(jnp.bfloat16)
        mixed, probs, rounded = attend(query, key_in, value_in)
        partial_value = jnp.dot(mixed, full_o, preferred_element_type=jnp.float32)
        summed = lax.psum_scatter(
            partial_value.astype(jnp.bfloat16), "tensor", scatter_dimension=1, tiled=True
        ).astype(jnp.float32)
        output = (inputs.astype(jnp.float32) + summed).astype(jnp.bfloat16)
        old_out = lax.dynamic_index_in_dim(copy_out, slot, 0, keepdims=False)
        sent = jnp.clip(
            (output.astype(jnp.float32) - old_out.astype(jnp.float32)) * inverse_next, -qmax, qmax
        ).astype(jnp.bfloat16)
        renewed = (old_out.astype(jnp.float32) + scale_next * sent.astype(jnp.float32)).astype(
            jnp.bfloat16
        )
        copy_out = lax.dynamic_update_index_in_dim(copy_out, renewed, slot, 0)
        if tick + 1 < ticks:
            passed = passed_along(sent, "section", 1)
        upstream = out_grad[0, tick, 0]
        d_mixed = lax.dot_general(
            upstream, full_o, (((1,), (1,)), ((), ())), preferred_element_type=jnp.float32
        ).astype(jnp.bfloat16)
        d_query, d_value = attend_back(query, key_in, value_in, probs, rounded, d_mixed)
        kept_normed.append(normed)
        kept_dq.append(d_query)
        kept_dv.append(d_value)
    rows_normed = jnp.concatenate(kept_normed, 0)
    rows_dq = jnp.concatenate(kept_dq, 0)
    rows_dv = jnp.concatenate(kept_dv, 0)
    term_q = local_term(rows_normed, rows_dq)
    term_v = local_term(rows_normed, rows_dv)
    grad_q, grad_v = (
        lax.psum_scatter(term_q.astype(jnp.bfloat16), "dp", scatter_dimension=0, tiled=True).astype(
            jnp.float32
        ),
        lax.psum_scatter(term_v.astype(jnp.bfloat16), "dp", scatter_dimension=0, tiled=True).astype(
            jnp.float32
        ),
    )
    copies_new = jnp.stack([copy_in, copy_out])[None]
    return (copies_new, grad_q.astype(jnp.bfloat16)[None], grad_v.astype(jnp.bfloat16)[None])


def solution(mesh):
    return jax.shard_map(
        on_device,
        mesh=mesh,
        in_specs=(
            P("section", None, "dp", None, "tensor"),
            P("section", "dp", None, "tensor"),
            P(None, "dp", None, "tensor"),
            P(None, "dp"),
            P(None, "tensor"),
            P("section", None),
            P("section", "dp", "tensor"),
            P("section", "dp", "tensor"),
            P("section", "dp", "tensor"),
            P("section", "tensor", "dp"),
            P("section", None, "dp", None, None),
        ),
        out_specs=(
            P("section", None, "dp", None, "tensor"),
            P("section", "dp", "tensor"),
            P("section", "dp", "tensor"),
        ),
        check_vma=False,
    )
```

profile of v0, /device:TPU:0, one launch (start us, length us, event | category | flops | bytes accessed | tf_op | source)
XLA Modules:
  0.0 630.1 jit_solution(12007615349595960774)
XLA Ops:
  10.7 2.3 slice_bitcast_fusion.1
  17.3 24.1 %all-gather.12.cloned.1.call-done = bf16[128,4096]{1,0:T(8,128)(2,1)} async-done(((bf16[128,1024]{1,0:T(8,128)(2,1)}), bf16[128,4096]{1,0:T(8,128)(2,1)}) %all-gather.12.cloned.1.call-update) | async-done | bytes 1048592 | tf_op jit(solution)/shard_map/all_gather | solution.py:115
  44.5 42.0 %all-gather.20.cloned.1.call-done = bf16[1,4096,128]{2,1,0:T(8,128)(2,1)} async-done(((bf16[1,256,128]{2,1,0:T(8,128)(2,1)}), bf16[1,4096,128]{2,1,0:T(8,128)(2,1)}) %all-gather.20.cloned.1.call-update) | async-done | bytes 1048592 | tf_op jit(solution)/shard_map/all_gather | solution.py:88
  88.2 42.4 %all-gather.18.cloned.1.call-done = bf16[1,4096,128]{2,1,0:T(8,128)(2,1)} async-done(((bf16[1,256,128]{2,1,0:T(8,128)(2,1)}), bf16[1,4096,128]{2,1,0:T(8,128)(2,1)}) %all-gather.18.cloned.1.call-update) | async-done | bytes 1048592 | tf_op jit(solution)/shard_map/all_gather | solution.py:89
  132.2 77.8 %all-gather.24.cloned.1.call-done = bf16[1,1024,4096]{2,1,0:T(8,128)(2,1)} async-done(((bf16[1,1024,256]{2,1,0:T(8,128)(2,1)}), bf16[1,1024,4096]{2,1,0:T(8,128)(2,1)}) %all-gather.24.cloned.1.call-update) | async-done | bytes 8388624 | tf_op jit(solution)/shard_map/all_gather | solution.py:90
  210.0 6.6 %fusion.48 = bf16[128,1024]{1,0:T(8,128)(2,1)S(1)} fusion(bf16[1,1024,4096]{2,1,0:T(8,128)(2,1)} %all-gather.24.cloned.1.call-done, bf16[1,3,1,128,4096]{4,3,2,1,0:T(8,128)(2,1)} %param.21), kind=kOutput, calls=%fused_computation.51 | convolution fusion | flops 1073872896 | bytes 9699328 | tf_op jit(solution)/shard_map/dot_general | solution.py:137
  216.9 65.2 %all-gather.22.cloned.1.call-done = bf16[1,4096,1024]{2,1,0:T(8,128)(2,1)} async-done(((bf16[1,256,1024]{2,1,0:T(8,128)(2,1)}), bf16[1,4096,1024]{2,1,0:T(8,128)(2,1)}) %all-gather.22.cloned.1.call-update) | async-done | bytes 8388624 | tf_op jit(solution)/shard_map/all_gather | solution.py:87
  282.1 4.6 fusion.66
  288.8 5.7 fusion.18
  294.6 23.5 %reduce-scatter.6.cloned.1.call-done = bf16[128,1024]{1,0:T(8,128)(2,1)} async-done(((bf16[128,4096]{1,0:T(8,128)(2,1)}), bf16[128,1024]{1,0:T(8,128)(2,1)}) %reduce-scatter.6.cloned.1.call-update) | async-done | bytes 262160 | tf_op jit(solution)/shard_map/reduce_scatter | solution.py:122
  323.8 2.0 fusion.117
  326.0 7.3 %fusion.51 = bf16[128,1024]{1,0:T(8,128)(2,1)} fusion(bf16[1,1024,4096]{2,1,0:T(8,128)(2,1)} %all-gather.24.cloned.1.call-done, bf16[1,3,1,128,4096]{4,3,2,1,0:T(8,128)(2,1)} %param.21), kind=kOutput, calls=%fused_computation.52 | convolution fusion | flops 1073872896 | bytes 9699328 | tf_op jit(solution)/shard_map/dot_general | solution.py:137
  333.4 16.4 %all-gather.14.cloned.1.call-done = bf16[128,4096]{1,0:T(8,128)(2,1)} async-done(((bf16[128,1024]{1,0:T(8,128)(2,1)}), bf16[128,4096]{1,0:T(8,128)(2,1)}) %all-gather.14.cloned.1.call-update) | async-done | bytes 1048592 | tf_op jit(solution)/shard_map/all_gather | solution.py:115
  354.1 5.1 fusion.63
  361.7 2.3 fusion.21
  364.8 23.5 %reduce-scatter.8.cloned.1.call-done = bf16[128,1024]{1,0:T(8,128)(2,1)} async-done(((bf16[128,4096]{1,0:T(8,128)(2,1)}), bf16[128,1024]{1,0:T(8,128)(2,1)}) %reduce-scatter.8.cloned.1.call-update) | async-done | bytes 262160 | tf_op jit(solution)/shard_map/reduce_scatter | solution.py:122
  388.3 2.1 fusion.139
  390.4 2.0 collective-permute-start.1
  394.4 1.8 bitcast_dynamic-update-slice_fusion
  397.4 7.3 %fusion.54 = bf16[128,1024]{1,0:T(8,128)(2,1)} fusion(bf16[1,1024,4096]{2,1,0:T(8,128)(2,1)} %all-gather.24.cloned.1.call-done, bf16[1,3,1,128,4096]{4,3,2,1,0:T(8,128)(2,1)} %param.21), kind=kOutput, calls=%fused_computation.53 | convolution fusion | flops 1073872896 | bytes 9699328 | tf_op jit(solution)/shard_map/dot_general | solution.py:137
  404.7 16.3 %all-gather.16.cloned.1.call-done = bf16[128,4096]{1,0:T(8,128)(2,1)} async-done(((bf16[128,1024]{1,0:T(8,128)(2,1)}), bf16[128,4096]{1,0:T(8,128)(2,1)}) %all-gather.16.cloned.1.call-update) | async-done | bytes 1048592 | tf_op jit(solution)/shard_map/all_gather | solution.py:115
  424.3 4.8 fusion.60
  432.2 2.3 fusion.24
  434.5 1.8 copy.48
  436.4 1.7 copy.69
  438.1 1.7 copy.68
  439.8 1.9 fusion.80
  442.8 1.9 fusion.79
  447.1 2.8 convolution_convert_fusion.1
  453.7 6.9 %convolution_convert_fusion = bf16[4096,1024]{1,0:T(8,128)(2,1)} fusion(bf16[128,4096]{1,0:T(8,128)(2,1)S(1)} %fusion.35, bf16[128,4096]{1,0:T(8,128)(2,1)S(1)} %fusion.32, bf16[128,4096]{1,0:T(8,128)(2,1)S(1)} %fusion.29, bf16[128,1024]{0,1:T(8,128)(2,1)S(1)} %bitcast.411, bf16[128,1024]{0,1:T(8,128)(2,1)S(1)} %bitcast.410, bf16[128,1024]{0,1:T(8,128)(2,1)S(1)} %bitcast.409), kind=kOutput, calls=%fused_computation.18 | convolution fusion | flops 3237216256 | bytes 12320768 | tf_op jit(solution)/shard_map/dot_general | solution.py:65
  464.0 71.2 %reduce-scatter.14.cloned.1.call-done = bf16[256,128]{1,0:T(8,128)(2,1)} async-done(((bf16[4096,128]{1,0:T(8,128)(2,1)}), bf16[256,128]{1,0:T(8,128)(2,1)}) %reduce-scatter.14.cloned.1.call-update) | async-done | bytes 65552 | tf_op jit(solution)/shard_map/reduce_scatter | solution.py:153
  535.1 88.1 %reduce-scatter.12.cloned.1.call-done = bf16[256,1024]{1,0:T(8,128)(2,1)} async-done(((bf16[4096,1024]{1,0:T(8,128)(2,1)}), bf16[256,1024]{1,0:T(8,128)(2,1)}) %reduce-scatter.12.cloned.1.call-update) | async-done | bytes 524304 | tf_op jit(solution)/shard_map/reduce_scatter | solution.py:150
  (165 shorter events, 43.8 us)
Async XLA Ops:
  7.2 6.5 %copy-start.29 = (bf16[1,1,128,1024]{3,2,1,0:T(8,128)(2,1)S(1)}, bf16[1,1,128,1024]{3,2,1,0:T(8,128)(2,1)}, u32[]{:S(2)}) copy-start(bf16[1,1,128,1024]{3,2,1,0:T(8,128)(2,1)} %param.12) | copy-start | bytes 786436
  7.2 34.2 %all-gather.12.cloned.1.call-start = ((), (), s32[]{:S(2)}) async-start(), calls=%async_computation.5 | async-start | bytes 1310720 | tf_op jit(solution)/shard_map/all_gather | solution.py:115
  10.7 32.2 %copy-start.30 = (f32[1,4096]{1,0:T(1,128)S(1)}, f32[1,4096]{1,0:T(1,128)}, u32[]{:S(2)}) copy-start(f32[1,4096]{1,0:T(1,128)} %param.16) | copy-start | bytes 49156
  13.0 29.9 %copy-start.27 = (bf16[1,1,2,128,1024]{4,3,2,1,0:T(8,128)(2,1)}, bf16[1,1,2,128,1024]{4,3,2,1,0:T(8,128)(2,1)S(1)}, u32[]{:S(2)}) copy-start(bf16[1,1,2,128,1024]{4,3,2,1,0:T(8,128)(2,1)S(1)} %get-tuple-element.12) | copy-start | bytes 1572868
  14.6 72.0 %all-gather.20.cloned.1.call-start = ((), (), s32[]{:S(2)}) async-start(), calls=%async_computation.14 | async-start | bytes 1114112 | tf_op jit(solution)/shard_map/all_gather | solution.py:88
  15.3 115.2 %all-gather.18.cloned.1.call-start = ((), (), s32[]{:S(2)}) async-start(), calls=%async_computation.13 | async-start | bytes 1114112 | tf_op jit(solution)/shard_map/all_gather | solution.py:89
  16.0 194.0 %all-gather.24.cloned.1.call-start = ((), (), s32[]{:S(2)}) async-start(), calls=%async_computation.16 | async-start | bytes 8912896 | tf_op jit(solution)/shard_map/all_gather | solution.py:90
  16.6 265.5 %all-gather.22.cloned.1.call-start = ((), (), s32[]{:S(2)}) async-start(), calls=%async_computation.15 | async-start | bytes 8912896 | tf_op jit(solution)/shard_map/all_gather | solution.py:87
  17.2 300.9 %reduce-scatter.6.cloned.1.call-start = ((), (), s32[]{:S(2)}) async-start(), calls=%async_computation.6 | async-start | bytes 1310720 | tf_op jit(solution)/shard_map/reduce_scatter | solution.py:122
  216.9 70.2 %copy-start.21 = (f32[1,8,128,128]{2,3,1,0:T(8,128)}, f32[1,8,128,128]{2,3,1,0:T(8,128)S(1)}, u32[]{:S(2)}) copy-start(f32[1,8,128,128]{2,3,1,0:T(8,128)S(1)} %convolution_bitcast_fusion.2) | copy-start | bytes 1572868
  287.8 6.7 %copy-start.31 = (f32[8,128]{1,0:T(8,128)}, f32[8,128]{1,0:T(8,128)S(1)}, u32[]{:S(2)}) copy-start(f32[8,128]{1,0:T(8,128)S(1)} %fusion.131) | copy-start | bytes 12292
  288.5 6.0 copy-start.16
  288.8 29.3 %copy-start.19 = (bf16[128,1024]{1,0:T(8,128)(2,1)S(1)}, bf16[128,1024]{1,0:T(8,128)(2,1)}, u32[]{:S(2)}) copy-start(bf16[128,1024]{1,0:T(8,128)(2,1)} %fusion.101) | copy-start | bytes 786436
  288.8 34.0 %copy-start.28 = (bf16[1,1,2,128,1024]{4,3,2,1,0:T(8,128)(2,1)S(1)}, bf16[1,1,2,128,1024]{4,3,2,1,0:T(8,128)(2,1)}, u32[]{:S(2)}) copy-start(bf16[1,1,2,128,1024]{4,3,2,1,0:T(8,128)(2,1)} %copy-done.27) | copy-start | bytes 1572868
  294.5 55.3 %all-gather.14.cloned.1.call-start = ((), (), s32[]{:S(2)}) async-start(), calls=%async_computation.7 | async-start | bytes 1310720 | tf_op jit(solution)/shard_map/all_gather | solution.py:115
  319.3 14.0 %copy-start.10 = (bf16[2,128,1024]{2,1,0:T(8,128)(2,1)}, bf16[2,128,1024]{2,1,0:T(8,128)(2,1)S(1)}, u32[]{:S(2)}) copy-start(bf16[2,128,1024]{2,1,0:T(8,128)(2,1)S(1)} %get-tuple-element.7) | copy-start | bytes 1572868
  319.3 4.5 collective-permute-start
  323.8 9.6 %copy-start.8 = (bf16[2,128,1024]{2,1,0:T(8,128)(2,1)}, bf16[2,128,1024]{2,1,0:T(8,128)(2,1)S(1)}, u32[]{:S(2)}) copy-start(bf16[2,128,1024]{2,1,0:T(8,128)(2,1)S(1)} %fusion.142) | copy-start | bytes 1572868
  325.8 62.5 %reduce-scatter.8.cloned.1.call-start = ((), (), s32[]{:S(2)}) async-start(), calls=%async_computation.8 | async-start | bytes 1310720 | tf_op jit(solution)/shard_map/reduce_scatter | solution.py:122
  333.4 19.6 %copy-start = (bf16[1,4096,128]{2,1,0:T(8,128)(2,1)S(1)}, bf16[1,4096,128]{2,1,0:T(8,128)(2,1)}, u32[]{:S(2)}) copy-start(bf16[1,4096,128]{2,1,0:T(8,128)(2,1)} %all-gather.18.cloned.1.call-done) | copy-start | bytes 3145732
  353.7 5.9 copy-start.22
  353.7 8.0 %slice-start = ((s8[8388608]{0:T(1024)(128)(4,1)}), s8[4194304]{0:T(1024)(128)(4,1)S(1)}, s32[]{:S(2)}) async-start(s8[8388608]{0:T(1024)(128)(4,1)} %bitcast.377), calls=%async_computation.17 | async-start | bytes 8388608
  354.1 7.6 %slice-start.1 = ((s8[8388608]{0:T(1024)(128)(4,1)}), s8[4194304]{0:T(1024)(128)(4,1)S(1)}, s32[]{:S(2)}) async-start(s8[8388608]{0:T(1024)(128)(4,1)} %bitcast.377), calls=%async_computation.18 | async-start | bytes 8388608
  361.7 26.6 %copy-start.9 = (bf16[2,128,1024]{2,1,0:T(8,128)(2,1)S(1)}, bf16[2,128,1024]{2,1,0:T(8,128)(2,1)}, u32[]{:S(2)}) copy-start(bf16[2,128,1024]{2,1,0:T(8,128)(2,1)} %copy-done.8) | copy-start | bytes 1572868
  364.0 57.0 %all-gather.16.cloned.1.call-start = ((), (), s32[]{:S(2)}) async-start(), calls=%async_computation.9 | async-start | bytes 1310720 | tf_op jit(solution)/shard_map/all_gather | solution.py:115
  390.4 14.3 %copy-start.12 = (bf16[2,128,1024]{2,1,0:T(8,128)(2,1)}, bf16[2,128,1024]{2,1,0:T(8,128)(2,1)S(1)}, u32[]{:S(2)}) copy-start(bf16[2,128,1024]{2,1,0:T(8,128)(2,1)S(1)} %get-tuple-element.5) | copy-start | bytes 1572868
  390.4 4.0 collective-permute-start.1
  397.1 64.6 %reduce-scatter.10.cloned.1.call-start = ((), (), s32[]{:S(2)}) async-start(), calls=%async_computation.10 | async-start | bytes 1310720 | tf_op jit(solution)/shard_map/reduce_scatter | solution.py:122
  422.5 9.6 %slice-start.2 = ((s8[8388608]{0:T(1024)(128)(4,1)}), s8[4194304]{0:T(1024)(128)(4,1)S(1)}, s32[]{:S(2)}) async-start(s8[8388608]{0:T(1024)(128)(4,1)} %bitcast.379), calls=%async_computation.19 | async-start | bytes 8388608
  424.3 7.9 %slice-start.3 = ((s8[8388608]{0:T(1024)(128)(4,1)}), s8[4194304]{0:T(1024)(128)(4,1)S(1)}, s32[]{:S(2)}) async-start(s8[8388608]{0:T(1024)(128)(4,1)} %bitcast.379), calls=%async_computation.20 | async-start | bytes 8388608
  434.5 100.7 %reduce-scatter.14.cloned.1.call-start = ((), (), s32[]{:S(2)}) async-start(), calls=%async_computation.12 | async-start | bytes 1114112 | tf_op jit(solution)/shard_map/reduce_scatter | solution.py:153
  449.9 173.4 %reduce-scatter.12.cloned.1.call-start = ((), (), s32[]{:S(2)}) async-start(), calls=%async_computation.11 | async-start | bytes 8912896 | tf_op jit(solution)/shard_map/reduce_scatter | solution.py:150
  (23 other events, 48.7 us)
Sparse Core Ops, SparseCore 0:
  14.7 26.6 all-gather.11
  43.5 42.9 all-gather.19
  88.7 41.8 all-gather.17
  132.5 77.4 all-gather.23
  212.0 70.0 all-gather.21
  294.6 23.3 reduce-scatter.5
  325.9 23.8 all-gather.13
  364.1 24.1 reduce-scatter.7
  397.2 23.7 all-gather.15
  434.6 24.1 reduce-scatter.9
  462.9 72.2 reduce-scatter.13
  539.0 84.1 reduce-scatter.11
where the time goes:
time: 631 us; the launch traced here: 630 us
  waiting for transfers between devices  493 us (78%)
  matrix products  71.2 us (11%)
  other arithmetic  23.3 us (4%)
  between operations  20.9 us (3%)
  local copies, waits for them, and re-layouts  17.1 us (3%)
    reduce_scatter x1, waiting for transfers between devices, on_device(): lax.psum_scatter(term_q.astype(jnp.bfloat16), 'dp', scatter_dimension=0,...  88.1 us
    all_gather x1, waiting for transfers between devices, on_device(): lax.all_gather(w_out[0], 'dp', axis=1, tiled=True)  77.8 us
    reduce_scatter x1, waiting for transfers between devices, on_device(): lax.psum_scatter(term_v.astype(jnp.bfloat16), 'dp', scatter_dimension=0,...  71.2 us
    all_gather x1, waiting for transfers between devices, on_device(): lax.all_gather(w_query[0], 'dp', axis=0, tiled=True)  65.2 us
    all_gather x3, waiting for transfers between devices, on_device(): whole = lax.all_gather(inputs, 'tensor', axis=1, tiled=True)  56.8 us
    reduce_scatter x3, waiting for transfers between devices, on_device(): lax.psum_scatter(partial_value.astype(jnp.bfloat16), 'tensor', scatter_di...  47 us
    all_gather x1, waiting for transfers between devices, on_device(): lax.all_gather(w_value[0], 'dp', axis=0, tiled=True)  42.4 us
    all_gather x1, waiting for transfers between devices, on_device(): lax.all_gather(w_key[0], 'dp', axis=0, tiled=True)  42 us
  transfers between devices with their start and end apart: 14, of which 11 were waited for; matrix products, arithmetic and copies ran while one was open for 9% of the time, Pallas kernels for 0%

commit v1 on v0

v1 whole, which is shorter than its diff:
```python
import jax
import jax.numpy as jnp
from jax import lax
from jax.sharding import Mesh, PartitionSpec as P

HQ = 32
HK = 4
HD = 128
QB = 128
SEQ = 128

eps_norm = 1e-05
qmax = 7.0
f32 = jnp.float32
bf16 = jnp.bfloat16


def normalize(inputs, gain):
    values = inputs.astype(f32)
    square = jnp.mean(values * values, axis=-1, keepdims=True)
    return (values * lax.rsqrt(square + eps_norm) * gain).astype(bf16)


def heads(rows, units):
    return rows.reshape(units, SEQ, -1, HD)


def softmax_probs(query, key_in, units):
    scores = (
        jnp.einsum(
            "usgd,utd->ugst",
            heads(query, units),
            key_in.reshape(units, SEQ, HD),
            preferred_element_type=f32,
        )
        * HD ** (-0.5)
    )
    causal = jnp.arange(SEQ)[:, None] >= jnp.arange(SEQ)[None, :]
    return jax.nn.softmax(jnp.where(causal, scores, -1e30), axis=-1)


def attend(query, key_in, value_in, units):
    rounded = softmax_probs(query, key_in, units).astype(bf16)
    mixed = jnp.einsum(
        "ugst,utd->usgd", rounded, value_in.reshape(units, SEQ, HD), preferred_element_type=f32
    )
    return mixed.reshape(units * SEQ, -1).astype(bf16)


def attend_back(query, key_in, value_in, d_mixed, units):
    probs = softmax_probs(query, key_in, units)
    d_heads = heads(d_mixed, units)
    d_probs = jnp.einsum(
        "usgd,utd->ugst", d_heads, value_in.reshape(units, SEQ, HD), preferred_element_type=f32
    )
    d_scores = probs * (d_probs - jnp.sum(d_probs * probs, axis=-1, keepdims=True)) * HD ** (-0.5)
    d_query = jnp.einsum(
        "ugst,utd->usgd",
        d_scores.astype(bf16),
        key_in.reshape(units, SEQ, HD),
        preferred_element_type=f32,
    )
    d_value = jnp.einsum("ugst,usgd->utd", probs.astype(bf16), d_heads, preferred_element_type=f32)
    return (
        d_query.reshape(units * SEQ, -1).astype(bf16),
        d_value.reshape(units * SEQ, HD).astype(bf16),
    )


def pick(state, slot):
    return jnp.where(slot == 0, state[0], state[1])


def put(state, slot, new, active=True):
    mask = (jnp.arange(2) == slot) & active
    return jnp.where(mask[:, None, None], new[None], state)


def pass_on(shard):
    return lax.ppermute(shard, "section", [(0, 1)])


def gather_tensor(shard):
    return lax.all_gather(shard, "tensor", axis=1, tiled=True)


def reduce_tensor(partial):
    rows = partial.shape[0]
    parts = partial.reshape(rows, 4, -1).swapaxes(0, 1)
    got = lax.all_to_all(parts, "tensor", split_axis=0, concat_axis=0, tiled=True)
    return jnp.sum(got.astype(f32), axis=0)


def on_device(
    boundary_copies,
    arriving,
    first_delta,
    sample_index,
    exponents,
    norm_gain,
    w_query,
    w_key,
    w_value,
    w_out,
    out_grad,
):
    section = lax.axis_index("section")
    first = section == 0
    packed = jnp.concatenate([w_query[0], w_key[0], w_value[0], w_out[0].T], axis=1)
    full = lax.all_gather(packed, ("y", "x"), axis=0, tiled=True)
    full_qkv = full[:, :1280]
    full_o = full[:, 1280:]

    power = exponents.astype(f32)
    scale_full = jnp.repeat(jnp.exp2(power), QB, axis=1)
    inverse_full = jnp.repeat(jnp.exp2(-power), QB, axis=1)
    scale_in = jnp.where(first, scale_full[0], scale_full[1])
    scale_next = jnp.where(first, scale_full[1], scale_full[2])
    inverse_next = jnp.where(first, inverse_full[1], inverse_full[2])
    gain = norm_gain[0]
    slots = sample_index[:, 0]
    slot = [jnp.where(first, slots[k + 1], slots[k]) for k in range(3)]

    def receive(state, at, delta):
        return (pick(state, at).astype(f32) + scale_in * delta.astype(f32)).astype(bf16)

    def deliver(state, at, inputs, summed):
        output = (inputs.astype(f32) + summed).astype(bf16)
        old = pick(state, at)
        sent = jnp.clip(
            (output.astype(f32) - old.astype(f32)) * inverse_next, -qmax, qmax
        ).astype(bf16)
        renewed = (old.astype(f32) + scale_next * sent.astype(f32)).astype(bf16)
        return sent, renewed

    state_in, state_out = boundary_copies[0, 0], boundary_copies[0, 1]
    xa0 = receive(state_in, slot[0], arriving[0, 0])
    state_in = put(state_in, slot[0], xa0)
    xa1 = receive(state_in, slot[1], first_delta[0, 0])
    state_in = put(state_in, slot[1], xa1, first)
    xa = jnp.concatenate([xa0, xa1], 0)
    normed_a = normalize(gather_tensor(xa), gain)
    qkv_a = jnp.dot(normed_a, full_qkv, preferred_element_type=f32).astype(bf16)
    mixed_a = attend(qkv_a[:, :1024], qkv_a[:, 1024:1152], qkv_a[:, 1152:], 2)
    partial_a = lax.dot_general(
        mixed_a, full_o, (((1,), (1,)), ((), ())), preferred_element_type=f32
    ).astype(bf16)
    summed_a = reduce_tensor(partial_a)
    sent_a0, renewed = deliver(state_out, slot[0], xa0, summed_a[:SEQ])
    state_out = put(state_out, slot[0], renewed)
    sent_a1, renewed = deliver(state_out, slot[1], xa1, summed_a[SEQ:])
    state_out = put(state_out, slot[1], renewed, first)
    passed = pass_on(jnp.concatenate([sent_a0, sent_a1], 0))

    at_b0 = jnp.where(first, slot[2], slot[1])
    xb0 = receive(state_in, at_b0, jnp.where(first, first_delta[1, 0], passed[:SEQ]))
    state_in = put(state_in, at_b0, xb0)
    xb1 = receive(state_in, slot[2], passed[SEQ:])
    state_in = put(state_in, slot[2], xb1, ~first)
    xb = jnp.concatenate([xb0, xb1], 0)
    normed_b = normalize(gather_tensor(xb), gain)
    qkv_b = jnp.dot(normed_b, full_qkv, preferred_element_type=f32).astype(bf16)
    mixed_b = attend(qkv_b[:, :1024], qkv_b[:, 1024:1152], qkv_b[:, 1152:], 2)
    partial_b = lax.dot_general(
        mixed_b, full_o, (((1,), (1,)), ((), ())), preferred_element_type=f32
    ).astype(bf16)
    summed_b = reduce_tensor(partial_b)
    _, renewed = deliver(state_out, at_b0, xb0, summed_b[:SEQ])
    state_out = put(state_out, at_b0, renewed)
    _, renewed = deliver(state_out, slot[2], xb1, summed_b[SEQ:])
    state_out = put(state_out, slot[2], renewed, ~first)

    up = out_grad[0, :, 0].reshape(3 * SEQ, -1)
    d_mixed = jnp.dot(up, full_o, preferred_element_type=f32).astype(bf16)
    d_mixed = jnp.concatenate(
        [
            d_mixed[:SEQ],
            jnp.where(first, d_mixed[SEQ : 2 * SEQ], d_mixed[2 * SEQ :]),
            jnp.where(first, d_mixed[2 * SEQ :], d_mixed[SEQ : 2 * SEQ]),
        ],
        0,
    )

    def three(a, b):
        return jnp.concatenate([a[:SEQ], jnp.where(first, a[SEQ:], b[SEQ:]), b[:SEQ]], 0)

    qkv = three(qkv_a, qkv_b)
    normed = three(normed_a, normed_b)
    d_query, d_value = attend_back(qkv[:, :1024], qkv[:, 1024:1152], qkv[:, 1152:], d_mixed, 3)
    d_rows = jnp.concatenate([d_query, d_value], 1)
    term = lax.dot_general(
        normed, d_rows, (((0,), (0,)), ((), ())), preferred_element_type=f32
    ).astype(bf16)
    grad = lax.psum_scatter(term, ("y", "x"), scatter_dimension=0, tiled=True)
    copies_new = jnp.stack([state_in, state_out])[None]
    return (copies_new, grad[None, :, :1024], grad[None, :, 1024:])


def solution(mesh):
    shape = dict(mesh.shape)
    grid = Mesh(
        mesh.devices.reshape(shape["section"], 4, shape["dp"] // 4, shape["tensor"]),
        ("section", "y", "x", "tensor"),
    )
    dp = ("y", "x")
    return jax.shard_map(
        on_device,
        mesh=grid,
        in_specs=(
            P("section", None, dp, None, "tensor"),
            P("section", dp, None, "tensor"),
            P(None, dp, None, "tensor"),
            P(None, dp),
            P(None, "tensor"),
            P("section", None),
            P("section", dp, "tensor"),
            P("section", dp, "tensor"),
            P("section", dp, "tensor"),
            P("section", "tensor", dp),
            P("section", None, dp, None, None),
        ),
        out_specs=(
            P("section", None, dp, None, "tensor"),
            P("section", dp, "tensor"),
            P("section", dp, "tensor"),
        ),
        check_vma=False,
    )
```

time: 631 us -> 408 us (0.65)
  waiting for transfers between devices: 493 us -> 274 us
  matrix products: 71.2 us -> 55.7 us
  local copies, waits for them, and re-layouts: 17.1 us -> 26.7 us
    reduce_scatter x5 -> x1, waiting for transfers between devices: 206 us -> 42.7 us  [on_device(): grad = lax.psum_scatter(term, ('y', 'x'), scatter_dimension=0, tiled=True)]
    all_gather x7 -> x3, waiting for transfers between devices: 284 us -> 180 us  [the longest x1 129 us: on_device(): full = lax.all_gather(packed, ('y', 'x'), axis=0, tiled=True)]
    all_to_all x0 -> x2, waiting for transfers between devices: none -> 51 us  [reduce_tensor(): lax.all_to_all(parts, 'tensor', split_axis=0, concat_axis=0, tiled=True)]
    dot_general x32 -> x13, matrix products: 71.2 us -> 51.9 us  [the longest x1 9.56 us: on_device(): lax.dot_general(normed, d_rows, (((0,), (0,)), ((), ())), preferred_eleme...]
    all_to_all x0 -> x2, starting transfers between devices: none -> 8.05 us  [reduce_tensor(): lax.all_to_all(parts, 'tensor', split_axis=0, concat_axis=0, tiled=True)]
    dynamic_update_slice x5 -> x0, other arithmetic: 7.37 us -> none  [the longest x3 4.48 us: on_device(): copy_out = lax.dynamic_update_index_in_dim(copy_out, renewed, slot, 0)]
    unnamed x90 -> x79, local copies, waits for them, and re-layouts: 8.57 us -> 13.1 us
  transfers between devices with their start and end apart: 14 -> 7, of which waited for: 11 -> 7; matrix products, arithmetic and copies ran while one was open for 9% -> 7% of each run, Pallas kernels for 0% -> 0%
where the time goes in v1:
time: 408 us; the launch traced here: 407 us
  waiting for transfers between devices  274 us (67%)
  matrix products  55.7 us (14%)
  local copies, waits for them, and re-layouts  26.7 us (7%)
  other arithmetic  23.3 us (6%)
  between operations  18.1 us (4%)
  starting transfers between devices  9.72 us (2%)
    all_gather x1, waiting for transfers between devices, on_device(): full = lax.all_gather(packed, ('y', 'x'), axis=0, tiled=True)  129 us
    all_to_all x2, waiting for transfers between devices, reduce_tensor(): lax.all_to_all(parts, 'tensor', split_axis=0, concat_axis=0, tiled=True)  51 us
    all_gather x2, waiting for transfers between devices, gather_tensor(): return lax.all_gather(shard, 'tensor', axis=1, tiled=True)  50.3 us
    reduce_scatter x1, waiting for transfers between devices, on_device(): grad = lax.psum_scatter(term, ('y', 'x'), scatter_dimension=0, tiled=True)  42.7 us
    unnamed x79, local copies, waits for them, and re-layouts  13.1 us
    dot_general x1, matrix products, on_device(): lax.dot_general(normed, d_rows, (((0,), (0,)), ((), ())), preferred_eleme...  9.56 us
  transfers between devices with their start and end apart: 7, of which 7 were waited for; matrix products, arithmetic and copies ran while one was open for 7% of the time, Pallas kernels for 0%

profile of v1, /device:TPU:0, one launch (start us, length us, event | category | flops | bytes accessed | tf_op | source)
XLA Modules:
  0.0 407.2 jit_solution(15412829864320131191)
XLA Ops:
  7.2 1.5 fusion.149
  18.1 2.0 copy.45
  20.2 2.3 pad_maximum_fusion
  22.6 28.1 %all-gather.4.cloned.1.call-done = bf16[256,4096]{1,0:T(8,128)(2,1)} async-done(((bf16[256,1024]{1,0:T(8,128)(2,1)}), bf16[256,4096]{1,0:T(8,128)(2,1)}) %all-gather.4.cloned.1.call-update) | async-done | bytes 2097168 | tf_op jit(solution)/shard_map/all_gather | solution.py:84
  50.7 2.2 fusion.20
  53.0 1.9 fusion.22
  54.9 129.4 %all-gather.6.cloned.1.call-done = bf16[4096,2304]{0,1:T(8,128)(2,1)} async-done(((bf16[256,2304]{0,1:T(8,128)(2,1)}), bf16[4096,2304]{0,1:T(8,128)(2,1)}) %all-gather.6.cloned.1.call-update) | async-done | bytes 18874384 | tf_op jit(solution)/shard_map/all_gather | solution.py:110
  184.3 7.5 %fusion.31 = bf16[256,1280]{1,0:T(8,128)(2,1)S(1)} fusion(bf16[256,4096]{1,0:T(8,128)(2,1)} %fusion.22, bf16[4096,2304]{0,1:T(8,128)(2,1)} %all-gather.6.cloned.1.call-done), kind=kOutput, calls=%fused_computation.34 | convolution fusion | flops 2684682240 | bytes 13238272 | tf_op jit(solution)/shard_map/dot_general | solution.py:143
  193.7 1.5 fusion.150
  195.2 2.3 fusion.54
  197.6 2.8 fusion.59
  200.4 2.1 copy.51
  202.5 5.9 %fusion.14 = bf16[256,4096]{1,0:T(8,128)(2,1)S(1)} fusion(bf16[4096,2304]{0,1:T(8,128)(2,1)} %all-gather.6.cloned.1.call-done, bf16[32,8,8,128]{3,2,1,0:T(8,128)(2,1)} %bitcast.282), kind=kOutput, calls=%fused_computation.19 | convolution fusion | flops 2148532224 | bytes 11010048 | tf_op jit(solution)/shard_map/dot_general | solution.py:145
  208.4 1.6 copy.126
  209.9 4.4 %all-to-all-start = ((bf16[4,256,1024]{2,1,0:T(8,128)(2,1)}), bf16[4,256,1024]{2,1,0:T(8,128)(2,1)}, u32[]{:S(2)}, u32[]{:S(2)}) async-start(bf16[4,256,1024]{2,1,0:T(8,128)(2,1)} %bitcast.267), calls=%async_computation | async-start | bytes 4194304 | tf_op jit(solution)/shard_map/all_to_all | solution.py:90
  215.7 24.5 %all-to-all-done = bf16[4,256,1024]{2,1,0:T(8,128)(2,1)} async-done(((bf16[4,256,1024]{2,1,0:T(8,128)(2,1)}), bf16[4,256,1024]{2,1,0:T(8,128)(2,1)}, u32[]{:S(2)}, u32[]{:S(2)}) %all-to-all-start) | async-done | bytes 2097184 | tf_op jit(solution)/shard_map/all_to_all | solution.py:90
  240.2 2.2 convert_reduce_fusion.1
  249.1 6.0 %fusion.56 = bf16[384,1024]{1,0:T(8,128)(2,1)S(1)} fusion(bf16[384,4096]{1,0:T(8,128)(2,1)S(1)} %bitcast.266, bf16[4096,2304]{0,1:T(8,128)(2,1)} %all-gather.6.cloned.1.call-done), kind=kOutput, calls=%fused_computation.60 | convolution fusion | flops 3221618688 | bytes 12320768 | tf_op jit(solution)/shard_map/dot_general | solution.py:174
  255.4 22.2 %all-gather.8.cloned.1.call-done = bf16[256,4096]{1,0:T(8,128)(2,1)} async-done(((bf16[256,1024]{1,0:T(8,128)(2,1)}), bf16[256,4096]{1,0:T(8,128)(2,1)}) %all-gather.8.cloned.1.call-update) | async-done | bytes 2097168 | tf_op jit(solution)/shard_map/all_gather | solution.py:84
  277.6 2.2 fusion.23
  281.4 1.8 fusion.144
  283.2 6.9 %fusion.34 = bf16[256,1280]{1,0:T(8,128)(2,1)S(1)} fusion(bf16[256,4096]{1,0:T(8,128)(2,1)S(1)} %fusion.25, bf16[4096,2304]{0,1:T(8,128)(2,1)} %all-gather.6.cloned.1.call-done), kind=kOutput, calls=%fused_computation.35 | convolution fusion | flops 2684682240 | bytes 13238272 | tf_op jit(solution)/shard_map/dot_general | solution.py:162
  291.4 1.8 fusion.156
  295.0 3.5 fusion.55
  298.5 1.7 copy.62
  300.4 9.6 %convolution_convert_fusion = bf16[4096,1152]{1,0:T(8,128)(2,1)} fusion(bf16[128,4096]{1,0:T(8,128)(2,1)} %get-tuple-element.9, bf16[128,4096]{1,0:T(8,128)(2,1)S(1)} %copy-done.30, bf16[128,4096]{1,0:T(8,128)(2,1)S(1)} %copy-done.29, bf16[384,128]{1,0:T(8,128)(2,1)S(1)} %bitcast.297, bf16[384,1024]{1,0:T(8,128)(2,1)S(1)} %bitcast.279), kind=kOutput, calls=%fused_computation.4 | convolution fusion | flops 3639803904 | bytes 13467648 | tf_op jit(solution)/shard_map/dot_general | solution.py:191
  313.5 5.9 %fusion.17 = bf16[256,4096]{1,0:T(8,128)(2,1)S(1)} fusion(bf16[4096,2304]{0,1:T(8,128)(2,1)} %all-gather.6.cloned.1.call-done, bf16[32,8,8,128]{3,2,1,0:T(8,128)(2,1)} %bitcast.281), kind=kOutput, calls=%fused_computation.20 | convolution fusion | flops 2148532224 | bytes 11010048 | tf_op jit(solution)/shard_map/dot_general | solution.py:164
  319.5 1.6 copy.125
  321.0 3.6 all-to-all-start.1
  324.7 26.5 %all-to-all-done.1 = bf16[4,256,1024]{2,1,0:T(8,128)(2,1)S(1)} async-done(((bf16[4,256,1024]{2,1,0:T(8,128)(2,1)}), bf16[4,256,1024]{2,1,0:T(8,128)(2,1)S(1)}, u32[]{:S(2)}, u32[]{:S(2)}) %all-to-all-start.1) | async-done | bytes 2097184 | tf_op jit(solution)/shard_map/all_to_all | solution.py:90
  354.6 42.7 %reduce-scatter.2.cloned.1.call-done = bf16[256,1152]{1,0:T(8,128)(2,1)} async-done(((bf16[4096,1152]{1,0:T(8,128)(2,1)}), bf16[256,1152]{1,0:T(8,128)(2,1)}) %reduce-scatter.2.cloned.1.call-update) | async-done | bytes 589840 | tf_op jit(solution)/shard_map/reduce_scatter | solution.py:194
  398.8 1.9 slice_bitcast_fusion.1
  (134 shorter events, 28.9 us)
Async XLA Ops:
  7.2 241.9 %copy-start = (bf16[1,3,1,128,4096]{4,3,2,1,0:T(8,128)(2,1)S(1)}, bf16[1,3,1,128,4096]{4,3,2,1,0:T(8,128)(2,1)}, u32[]{:S(2)}) copy-start(bf16[1,3,1,128,4096]{4,3,2,1,0:T(8,128)(2,1)} %param.21) | copy-start | bytes 9437188
  7.2 43.5 %all-gather.4.cloned.1.call-start = ((), (), s32[]{:S(2)}) async-start(), calls=%async_computation.3 | async-start | bytes 2621440 | tf_op jit(solution)/shard_map/all_gather | solution.py:84
  11.2 4.1 %copy-start.27 = (bf16[2,1,128,1024]{3,2,1,0:T(8,128)(2,1)S(1)}, bf16[2,1,128,1024]{3,2,1,0:T(8,128)(2,1)}, u32[]{:S(2)}) copy-start(bf16[2,1,128,1024]{3,2,1,0:T(8,128)(2,1)} %param.13) | copy-start | bytes 1572868
  13.3 3.8 copy-start.32
  17.0 167.3 %all-gather.6.cloned.1.call-start = ((), (), s32[]{:S(2)}) async-start(), calls=%async_computation.4 | async-start | bytes 20054016 | tf_op jit(solution)/shard_map/all_gather | solution.py:110
  22.5 30.4 %copy-start.31 = (f32[1,4096]{1,0:T(1,128)S(1)}, f32[1,4096]{1,0:T(1,128)}, u32[]{:S(2)}) copy-start(f32[1,4096]{1,0:T(1,128)} %param.16) | copy-start | bytes 49156
  50.7 2.3 copy-start.4
  209.9 30.3 %all-to-all-start = ((bf16[4,256,1024]{2,1,0:T(8,128)(2,1)}), bf16[4,256,1024]{2,1,0:T(8,128)(2,1)}, u32[]{:S(2)}, u32[]{:S(2)}) async-start(bf16[4,256,1024]{2,1,0:T(8,128)(2,1)} %bitcast.267), calls=%async_computation | async-start | bytes 4194304 | tf_op jit(solution)/shard_map/all_to_all | solution.py:90
  214.4 63.2 %all-gather.8.cloned.1.call-start = ((), (), s32[]{:S(2)}) async-start(), calls=%async_computation.5 | async-start | bytes 2621440 | tf_op jit(solution)/shard_map/all_gather | solution.py:84
  240.2 2.2 copy-start.2
  242.6 2.5 copy-start.13
  242.6 2.3 copy-start.12
  242.6 2.3 copy-start.28
  243.5 2.6 copy-start.23
  243.6 2.8 collective-permute-start
  245.1 1.5 copy-start.25
  248.9 148.5 %reduce-scatter.2.cloned.1.call-start = ((), (), s32[]{:S(2)}) async-start(), calls=%async_computation.6 | async-start | bytes 10027008 | tf_op jit(solution)/shard_map/reduce_scatter | solution.py:194
  277.6 2.2 copy-start.5
  279.8 1.6 copy-start.6
  283.2 7.0 %copy-start.18 = (bf16[256,1280]{1,0:T(8,128)(2,1)S(1)}, bf16[256,1280]{1,0:T(8,128)(2,1)}, u32[]{:S(2)}) copy-start(bf16[256,1280]{1,0:T(8,128)(2,1)} %copy-done.17) | copy-start | bytes 1966084
  293.2 1.4 copy-start.33
  298.5 1.9 copy-start.29
  298.5 1.9 copy-start.30
  321.0 30.2 %all-to-all-start.1 = ((bf16[4,256,1024]{2,1,0:T(8,128)(2,1)}), bf16[4,256,1024]{2,1,0:T(8,128)(2,1)S(1)}, u32[]{:S(2)}, u32[]{:S(2)}) async-start(bf16[4,256,1024]{2,1,0:T(8,128)(2,1)} %bitcast.268), calls=%async_computation.1 | async-start | bytes 4194304 | tf_op jit(solution)/shard_map/all_to_all | solution.py:90
  324.6 27.0 %copy-start.8 = (bf16[128,1024]{1,0:T(8,128)(2,1)S(1)}, bf16[128,1024]{1,0:T(8,128)(2,1)}, u32[]{:S(2)}) copy-start(bf16[128,1024]{1,0:T(8,128)(2,1)} %copy-done.7) | copy-start | bytes 786436
  324.6 27.0 %copy-start.10 = (bf16[2,128,1024]{2,1,0:T(8,128)(2,1)S(1)}, bf16[2,128,1024]{2,1,0:T(8,128)(2,1)}, u32[]{:S(2)}) copy-start(bf16[2,128,1024]{2,1,0:T(8,128)(2,1)} %get-tuple-element.28) | copy-start | bytes 1572868
  351.6 1.3 copy-start.3
  351.6 1.3 copy-start.9
  351.6 1.4 copy-start.14
  351.6 1.5 copy-start.24
  351.6 1.6 copy-start.26
  353.2 47.5 %copy-start.1 = (bf16[1,3,1,128,4096]{4,3,2,1,0:T(8,128)(2,1)S(1)}, bf16[1,3,1,128,4096]{4,3,2,1,0:T(8,128)(2,1)}, u32[]{:S(2)}) copy-start(bf16[1,3,1,128,4096]{4,3,2,1,0:T(8,128)(2,1)} %param.21) | copy-start | bytes 9437188
  (9 other events, 7.7 us)
Sparse Core Ops, SparseCore 0:
  17.1 33.5 all-gather.3
  52.8 131.4 all-gather.5
  249.0 28.5 all-gather.7
  310.1 87.2 reduce-scatter.1
